TPU v7x, 32 devices: a whole 2x2x4 slice. The times are simulated.
32 devices in a mesh: subj: 8 (over z, core), vox: 4 (over y, x).
Axes of the slice: x: 2, y: 2, z: 4, core: 2. Of those that a mesh axis runs over, the one named last changes fastest.
Arguments:
- data: bfloat16 [16, 240, 16384], P('subj', None, 'vox'), may hold values from -40 to 40, as said below
- shared_start: bfloat16 [128, 240], replicated, may hold values from -6 to 6
Outputs:
- projections: float32 [16, 128, 240], P('subj')
- response: float32 [128, 240], replicated
Inputs may be any that keep to these rules, and one draw needn't show every extreme that they name: `data`: real-valued recordings.
All inputs are finite; a program needn't handle non-finite values.
Results may differ from a plain program's by a relative error of at most 0.00035.
The roundings to bfloat16 on the way count: a program that leaves them out, or rounds other values in their place, can miss the bound.
Values may be sent and summed in bfloat16 or wider, within the bound.
A program may use at most 64 MiB of HBM per device.

v0:
```python
import jax
import jax.numpy as jnp
from jax import lax
from jax.sharding import PartitionSpec as P

ITERS = 3
OUTER = 2


def polar_factor(first, squares):
    features = first.shape[1]
    identity = jnp.broadcast_to(jnp.eye(features, dtype=jnp.float32), first.shape)
    factor = identity
    for count in range(ITERS):
        inner = jnp.einsum("sik,sij->skj", factor, first, precision=lax.Precision.HIGHEST)
        gram = (
            jnp.einsum("skj,sjl->skl", inner, factor, precision=lax.Precision.HIGHEST)
            / squares[:, None, None]
        )
        factor = jnp.einsum(
            "sik,skj->sij", factor, 1.5 * identity - 0.5 * gram, precision=lax.Precision.HIGHEST
        )
    return factor


def from_frames(frame_gram, shared):
    subjects = frame_gram.shape[0] * lax.axis_size("subj")
    frames = frame_gram.shape[1]
    width = frames // lax.axis_size("vox")
    start = lax.axis_index("vox") * width
    shared_wide = shared.astype(jnp.float32)
    left = jnp.einsum("kt,stu->sku", shared_wide, frame_gram, precision=lax.Precision.HIGHEST)
    first = jnp.einsum("sku,ju->skj", left, shared_wide, precision=lax.Precision.HIGHEST)
    squares = jnp.trace(first, axis1=1, axis2=2) + 1e-06
    factor = polar_factor(first, squares)
    left_share = lax.dynamic_slice_in_dim(left, start, width, 2)
    share = (
        jnp.einsum("sik,sit->skt", factor, left_share, precision=lax.Precision.HIGHEST)
        / jnp.sqrt(squares)[:, None, None]
    )
    total = lax.psum(jnp.sum(share, axis=0), "subj") / jnp.float32(subjects)
    projections, response = (
        lax.all_gather(share, "vox", axis=2, tiled=True),
        lax.all_gather(total, "vox", axis=1, tiled=True),
    )
    return (projections, response)


def local(data, shared_start):
    shared = shared_start
    projections = None
    response = None
    frame_gram = lax.psum(
        jnp.einsum("stv,suv->stu", data, data, preferred_element_type=jnp.float32), "vox"
    )
    for outer in range(OUTER):
        projections, response = from_frames(frame_gram, shared)
        shared = response.astype(jnp.bfloat16)
    return (projections, response)


def solution(mesh):
    placed = (P("subj", None, "vox"), P())
    return jax.shard_map(
        local, mesh=mesh, in_specs=placed, out_specs=(P("subj", None, None), P()), check_vma=False
    )
```

profile of v0, /device:TPU:0, one launch (start us, length us, event | category | flops | bytes accessed | tf_op | source)
XLA Modules:
  0.0 157.0 jit_solution(11667415162260468533)
XLA Ops:
  7.2 5.3 %fusion.39 = f32[2,240,240]{2,1,0:T(8,128)} fusion(bf16[2,240,4096]{2,1,0:T(8,128)(2,1)} %param.2), kind=kOutput, calls=%fused_computation.54 | convolution fusion | flops 943718400 | bytes 4392960 | tf_op jit(solution)/shard_map/stv,suv->stu/dot_general | solution.py:54
  12.6 47.9 %all-reduce.2.cloned.1.call-done = f32[2,240,240]{2,1,0:T(8,128)} async-done(((f32[2,240,240]{2,1,0:T(8,128)}), f32[2,240,240]{2,1,0:T(8,128)}) %all-reduce.2.cloned.1.call-update) | async-done | bytes 460816 | tf_op jit(solution)/shard_map/psum | solution.py:53
  60.5 1.7 %fusion.30 = f32[2,240,128]{2,1,0:T(8,128)S(1)} fusion(f32[2,240,240]{2,1,0:T(8,128)} %all-reduce.2.cloned.1.call-done, bf16[128,240]{0,1:T(8,128)(2,1)S(1)} %copy-done), kind=kOutput, calls=%fused_computation.41 | convolution fusion | flops 176947200 | bytes 768000 | tf_op jit(solution)/shard_map/kt,stu->sku/dot_general | solution.py:32
  62.2 0.5 select_reduce_fusion.1
  62.7 0.4 fusion.27
  63.1 0.3 fusion.11
  63.4 0.3 fusion.24
  63.6 0.4 fusion.40
  64.0 0.3 fusion.9
  64.3 0.3 fusion.41
  64.6 0.4 fusion.42
  65.0 0.3 fusion.7
  65.3 0.3 fusion.43
  65.8 28.4 %psum.22 = f32[128,60]{0,1:T(8,128)S(1)} all-reduce(f32[128,60]{0,1:T(8,128)S(1)} %fusion.12), channel_id=1, replica_groups=mesh['subj'=8,'vox'=4] {'subj'}, use_global_device_ids=true, to_apply=%region_3.4 | all-reduce | flops 7680 | bytes 61440 | tf_op jit(solution)/shard_map/psum | solution.py:41
  94.2 7.9 %all-gather = bf16[4,60,128]{2,1,0:T(8,128)(2,1)S(1)} all-gather(bf16[1,60,128]{2,1,0:T(8,128)(2,1)S(1)} %multiply_bitcast_fusion.1), channel_id=1, replica_groups=mesh['subj'=8,'vox'=4] {'vox'}, dimensions={0}, use_global_device_ids=true | all-gather | bytes 76800 | tf_op jit(solution)/shard_map/all_gather | solution.py:44
  102.1 0.6 fusion.44
  102.7 0.5 select_reduce_fusion
  103.2 0.4 fusion.22
  103.6 0.3 fusion.5
  103.9 0.3 fusion.19
  104.2 0.4 fusion.45
  104.6 0.3 fusion.3
  104.8 0.3 fusion.46
  105.1 0.4 fusion.47
  105.5 0.3 fusion.1
  105.8 0.3 fusion.48
  106.1 0.3 fusion.38
  106.4 8.3 %all_gather.10 = f32[2,128,240]{1,0,2:T(2,128)S(1)} all-gather(f32[2,128,60]{1,0,2:T(2,128)S(1)} %copy.16), channel_id=1, replica_groups=mesh['subj'=8,'vox'=4] {'vox'}, dimensions={2}, use_global_device_ids=true | all-gather | bytes 307200 | tf_op jit(solution)/shard_map/all_gather | solution.py:43
  114.7 0.7 copy.17
  115.4 25.9 %psum.23 = f32[128,60]{0,1:T(8,128)S(1)} all-reduce(f32[128,60]{0,1:T(8,128)S(1)} %get-tuple-element.12), channel_id=1, replica_groups=mesh['subj'=8,'vox'=4] {'subj'}, use_global_device_ids=true, to_apply=%region_6.7 | all-reduce | flops 7680 | bytes 61440 | tf_op jit(solution)/shard_map/psum | solution.py:41
  141.3 8.1 %all-gather.1 = f32[4,60,128]{2,1,0:T(8,128)S(1)} all-gather(f32[1,60,128]{2,1,0:T(8,128)S(1)} %multiply_bitcast_fusion), channel_id=1, replica_groups=mesh['subj'=8,'vox'=4] {'vox'}, dimensions={0}, use_global_device_ids=true | all-gather | bytes 153600 | tf_op jit(solution)/shard_map/all_gather | solution.py:44
  149.5 0.7 reshape.19
  (16 shorter events, 0.5 us)
Async XLA Ops:
  7.2 53.3 %copy-start = (bf16[128,240]{0,1:T(8,128)(2,1)S(1)}, bf16[128,240]{0,1:T(8,128)(2,1)}, u32[]{:S(2)}) copy-start(bf16[128,240]{0,1:T(8,128)(2,1)} %param.3) | copy-start | bytes 184324
  7.2 53.3 %all-reduce.2.cloned.1.call-start = ((), (), s32[]{:S(2)}) async-start(), calls=%async_computation | async-start | bytes 983040 | tf_op jit(solution)/shard_map/psum | solution.py:53
  60.5 41.6 %copy-start.1 = (f32[2,240,240]{2,1,0:T(8,128)S(1)}, f32[2,240,240]{2,1,0:T(8,128)}, u32[]{:S(2)}) copy-start(f32[2,240,240]{2,1,0:T(8,128)} %all-reduce.2.cloned.1.call-done) | copy-start | bytes 1382404
Sparse Core Ops, SparseCore 0:
  12.7 47.7 all-reduce.1
where the time goes:
time: 157 us
  blocking collectives  78.7 us (50%)
  waiting for transfers between devices  47.9 us (31%)
  matrix products  14.6 us (9%)
  between operations  14.2 us (9%)
    psum x2, blocking collectives, from_frames(): total = lax.psum(jnp.sum(share, axis=0), 'subj') / jnp.float32(subjects)  54.3 us
    psum x1, waiting for transfers between devices, local(): lax.psum(jnp.einsum('stv,suv->stu', data, data, preferred_element_type=jn...  47.9 us
    all_gather x2, blocking collectives, from_frames(): lax.all_gather(total, 'vox', axis=1, tiled=True)  16.1 us
    all_gather x1, blocking collectives, from_frames(): lax.all_gather(share, 'vox', axis=2, tiled=True)  8.32 us
    dot_general x1, matrix products, local(): jnp.einsum('stv,suv->stu', data, data, preferred_element_type=jnp.float32)  5.31 us
  transfers between devices with their start and end apart: 1, of which 1 were waited for; matrix products, arithmetic and copies ran while one was open for 0% of the time, Pallas kernels for 0%

commit v1 on v0

v1 whole, which is shorter than its diff:
```python
import functools

import jax
import jax.numpy as jnp
from jax import lax
from jax.experimental import pallas as pl
from jax.experimental.pallas import tpu as pltpu
from jax.sharding import PartitionSpec as P

OUTER = 2
LANES = 128
ROWS = 16
PIECES = 4
MESH = pl.DeviceIdType.MESH


def each(start, stop, body):
    if stop - start <= 16:
        for step in range(start, stop):
            body(step)
    else:

        def looped(step, carry):
            body(step)
            return carry

        lax.fori_loop(start, stop, looped, 0)


def halves(x):
    high = x.astype(jnp.bfloat16)
    low = (x - high.astype(jnp.float32)).astype(jnp.bfloat16)
    return high, low


def dot(x, y):
    return jnp.dot(x, y, preferred_element_type=jnp.float32)


def dot_t(x, y):
    return lax.dot_general(x, y, (((1,), (1,)), ((), ())), preferred_element_type=jnp.float32)


def product(x, y):
    x_high, x_low = x
    y_high, y_low = y
    wide = jnp.concatenate([x_high, x_low], axis=1)
    tall = jnp.concatenate([y_high, y_high], axis=0)
    return dot(wide, tall) + dot(x_high, y_low)


def chain(shared, grams):
    features = shared.shape[0]
    row = lax.broadcasted_iota(jnp.int32, (features, features), 0)
    col = lax.broadcasted_iota(jnp.int32, (features, features), 1)
    left = [dot(shared, high) + dot(shared, low) for high, low in grams]
    left2 = [halves(x) for x in left]
    first = [dot_t(high, shared) + dot_t(low, shared) for high, low in left2]
    squares = [jnp.sum(jnp.where(row == col, x, 0.0), keepdims=True) + 1e-06 for x in first]
    gram = [x * (1.0 / s) for x, s in zip(first, squares)]
    gram2 = [halves(x) for x in gram]
    for last in (False, False, True):
        if not last:
            square = [product(x, x) for x in gram2]
        left = [1.5 * x - 0.5 * product(g, y) for x, g, y in zip(left, gram2, left2)]
        if not last:
            square2 = [halves(x) for x in square]
            gram = [
                2.25 * g - 1.5 * q + 0.25 * product(g2, q2)
                for g, q, g2, q2 in zip(gram, square, gram2, square2)
            ]
            gram2 = [halves(x) for x in gram]
            left2 = [halves(x) for x in left]
    return [x * lax.rsqrt(s) for x, s in zip(left, squares)]


def pack(gram, frames, total_rows):
    rest = frames - LANES
    row = lax.broadcasted_iota(jnp.int32, (LANES, LANES), 0)
    col = lax.broadcasted_iota(jnp.int32, (LANES, LANES), 1)
    corner = gram[LANES:, LANES:]
    corner = jnp.concatenate([corner, jnp.zeros((rest, LANES - rest), jnp.float32)], axis=1)
    corner = jnp.concatenate([corner, jnp.zeros((LANES - rest, LANES), jnp.float32)], axis=0)
    corner = pltpu.roll(corner, 1, 1)
    parts = [jnp.where(row >= col, gram[:LANES, :LANES], corner), gram[LANES:, :LANES]]
    if total_rows > frames:
        parts.append(jnp.zeros((total_rows - frames, LANES), jnp.float32))
    return jnp.concatenate(parts, axis=0)


def unpack(packed, frames):
    rest = frames - LANES
    row = lax.broadcasted_iota(jnp.int32, (LANES, LANES), 0)
    col = lax.broadcasted_iota(jnp.int32, (LANES, LANES), 1)
    both = packed[:LANES]
    cross = packed[LANES:frames]
    cross = jnp.concatenate([cross, jnp.zeros((LANES - rest, LANES), jnp.float32)], axis=0)
    top = jnp.where(row >= col, both, both.T)
    rolled = pltpu.roll(both, LANES - 1, 1)
    corner = jnp.where(col >= row, rolled, rolled.T)
    corner = jnp.where((row < rest) & (col < rest), corner, 0.0)
    return jnp.concatenate(
        [jnp.concatenate([top, cross.T], axis=1), jnp.concatenate([cross, corner], axis=1)], axis=0
    )


def kernel(
    cores, subj_n, vox_n, chunk, subjects,
    data_ref, shared_ref, proj_ref, resp_ref,
    held, acc, packed, parts, gathered, tiles, sums, shares, pieces, proj_buf,
    load_sem, out_sem, rs_send, rs_recv, ag_send, ag_recv, sum_send, sum_recv, share_send, share_recv,
    piece_send, piece_recv,
):
    own, frames, voxels = data_ref.shape
    features = shared_ref.shape[0]
    s = lax.axis_index("subj")
    v = lax.axis_index("vox")
    z = s // cores
    core = s % cores
    planes = subj_n // cores
    chips = planes * vox_n
    chip = z * vox_n + v
    tile_n = (features // ROWS) * 2
    mine = chip

    def subj_device(step):
        return (lax.rem(s + step, subj_n), v)

    def chip_device(step):
        other = lax.rem(chip + step, chips)
        return (other // vox_n * cores + core, lax.rem(other, vox_n))

    def vox_device(step):
        return (s, lax.rem(v + step, vox_n))

    width = voxels // PIECES
    loads = []
    for i in range(own):
        for p in range(PIECES):
            cut = pl.ds(p * width, width)
            load = pltpu.make_async_copy(
                data_ref.at[i, :, cut], held.at[i, :, cut], load_sem.at[i, p]
            )
            load.start()
            loads.append(load)

    barrier = pltpu.get_barrier_semaphore()

    def greet_subj(step):
        pl.semaphore_signal(barrier, inc=1, device_id=subj_device(step), device_id_type=MESH)

    def greet_chip(step):
        pl.semaphore_signal(barrier, inc=1, device_id=chip_device(step), device_id_type=MESH)

    each(1, subj_n, greet_subj)
    each(1, chips, greet_chip)

    def scatter(i, step):
        other = lax.rem(v + step, vox_n)
        return pltpu.make_async_remote_copy(
            src_ref=packed.at[i, pl.ds(pl.multiple_of(other * chunk, 8), chunk)],
            dst_ref=parts.at[i, step - 1],
            send_sem=rs_send.at[i, step - 1],
            recv_sem=rs_recv.at[i, step - 1],
            device_id=vox_device(step),
            device_id_type=MESH,
        )

    def gather(i, step):
        cut = pl.ds(pl.multiple_of(v * chunk, 8), chunk)
        return pltpu.make_async_remote_copy(
            src_ref=gathered.at[i, cut],
            dst_ref=gathered.at[i, cut],
            send_sem=ag_send.at[i, step - 1],
            recv_sem=ag_recv.at[i, step - 1],
            device_id=vox_device(step),
            device_id_type=MESH,
        )

    def sum_copy(o, step):
        other = lax.rem(s + step, subj_n)
        tile = jnp.minimum(other // cores * vox_n + v, tile_n - 1)
        return pltpu.make_async_remote_copy(
            src_ref=tiles.at[o, tile],
            dst_ref=sums.at[o, s],
            send_sem=sum_send.at[o, step - 1],
            recv_sem=sum_recv.at[o, step - 1],
            device_id=subj_device(step),
            device_id_type=MESH,
        )

    def share_copy(o, step):
        ref = pieces if o else shares
        tile = jnp.minimum(mine, tile_n - 1)
        return pltpu.make_async_remote_copy(
            src_ref=ref.at[tile],
            dst_ref=ref.at[tile],
            send_sem=(piece_send if o else share_send).at[step - 1],
            recv_sem=(piece_recv if o else share_recv).at[step - 1],
            device_id=chip_device(step),
            device_id_type=MESH,
        )

    def when(condition, body):
        if chips <= tile_n:
            body()
        else:
            pl.when(condition)(body)

    for i in range(own):
        for p in range(PIECES):
            loads[i * PIECES + p].wait()
            piece = held[i, :, p * width : (p + 1) * width]
            if p == 0:
                acc[...] = dot_t(piece, piece)
            else:
                acc[...] += dot_t(piece, piece)
        packed[i] = pack(acc[...], frames, vox_n * chunk)
        if i == 0:
            pl.semaphore_wait(barrier, subj_n - 1 + chips - 1)
        each(1, vox_n, lambda step: scatter(i, step).start())

    for i in range(own):
        each(1, vox_n, lambda step: scatter(i, step).wait_recv())
        total = packed[i, pl.ds(pl.multiple_of(v * chunk, 8), chunk)]
        for step in range(1, vox_n):
            total = total + parts[i, step - 1]
        gathered[i, pl.ds(pl.multiple_of(v * chunk, 8), chunk)] = total
        each(1, vox_n, lambda step: gather(i, step).start())

    grams = []
    for i in range(own):
        each(1, vox_n, lambda step: gather(i, step).wait_recv())
        grams.append(halves(unpack(gathered[i], frames)))

    shared = shared_ref[...]
    pad = jnp.zeros((features, 2 * LANES - frames), jnp.bfloat16)
    shared = jnp.concatenate([shared, pad], axis=1)

    for o in range(OUTER):
        projections = chain(shared, grams)
        total = projections[0]
        for other in projections[1:]:
            total = total + other
        for j in range(tile_n):
            tiles[o, j] = total[
                j // 2 * ROWS : (j // 2 + 1) * ROWS, j % 2 * LANES : (j % 2 + 1) * LANES
            ]

        def send_sum(step):
            other = lax.rem(s + step, subj_n)
            when(
                other // cores * vox_n + v < tile_n,
                lambda: sum_copy(o, step).start(),
            )

        each(1, subj_n, send_sum)
        if o == OUTER - 1:
            for i in range(own):
                proj_buf[i] = projections[i][:, :frames]
            writing = pltpu.make_async_copy(proj_buf, proj_ref, out_sem)
            writing.start()

        def reduce():
            sums[o, s] = tiles[o, mine]
            each(1, subj_n, lambda step: sum_copy(o, step).wait_recv())
            summed = sums[o, 0]
            for q in range(1, subj_n):
                summed = summed + sums[o, q]
            mean = summed / jnp.float32(subjects)
            if o == OUTER - 1:
                pieces[mine] = mean
            else:
                shares[mine] = mean.astype(jnp.bfloat16)
            each(1, chips, lambda step: share_copy(o, step).start())

        when(mine < tile_n, reduce)

        def wait_share(step):
            other = lax.rem(chip + chips - step, chips)
            when(other < tile_n, lambda: share_copy(o, step).wait_recv())

        each(1, chips, wait_share)
        ref = pieces if o == OUTER - 1 else shares
        shared = jnp.concatenate(
            [
                jnp.concatenate([ref[2 * a], ref[2 * a + 1]], axis=1)
                for a in range(tile_n // 2)
            ],
            axis=0,
        )
    resp_ref[...] = shared[:, :frames]

    for i in range(own):
        each(1, vox_n, lambda step: scatter(i, step).wait_send())
        each(1, vox_n, lambda step: gather(i, step).wait_send())
    for o in range(OUTER):

        def sent_sum(step):
            other = lax.rem(s + step, subj_n)
            when(
                other // cores * vox_n + v < tile_n,
                lambda: sum_copy(o, step).wait_send(),
            )

        each(1, subj_n, sent_sum)
        when(
            mine < tile_n,
            lambda: each(1, chips, lambda step: share_copy(o, step).wait_send()),
        )
    writing.wait()


def local(subj_n, vox_n, data, shared_start):
    own, frames, voxels = data.shape
    features = shared_start.shape[0]
    cores = 2
    chips = subj_n // cores * vox_n
    tile_n = features // ROWS * 2
    assert chips >= tile_n and tile_n % vox_n == 0
    chunk = -(-frames // (8 * vox_n)) * 8
    hbm = pl.BlockSpec(memory_space=pltpu.HBM)
    vmem = pl.BlockSpec(memory_space=pltpu.VMEM)
    f32, bf16 = jnp.float32, jnp.bfloat16
    dma = pltpu.SemaphoreType.DMA
    flops = 2 * own * frames * frames * voxels
    return pl.pallas_call(
        functools.partial(kernel, cores, subj_n, vox_n, chunk, own * subj_n),
        out_shape=(
            jax.ShapeDtypeStruct((own, features, frames), f32),
            jax.ShapeDtypeStruct((features, frames), f32),
        ),
        in_specs=[hbm, vmem],
        out_specs=(hbm, vmem),
        scratch_shapes=[
            pltpu.VMEM((own, frames, voxels), bf16),
            pltpu.VMEM((frames, frames), f32),
            pltpu.VMEM((own, vox_n * chunk, LANES), f32),
            pltpu.VMEM((own, vox_n - 1, chunk, LANES), f32),
            pltpu.VMEM((own, vox_n * chunk, LANES), f32),
            pltpu.VMEM((OUTER, tile_n, ROWS, LANES), f32),
            pltpu.VMEM((OUTER, subj_n, ROWS, LANES), f32),
            pltpu.VMEM((tile_n, ROWS, LANES), bf16),
            pltpu.VMEM((tile_n, ROWS, LANES), f32),
            pltpu.VMEM((own, features, frames), f32),
            dma((own, PIECES)),
            dma,
            dma((own, vox_n - 1)),
            dma((own, vox_n - 1)),
            dma((own, vox_n - 1)),
            dma((own, vox_n - 1)),
            dma((OUTER, subj_n - 1)),
            dma((OUTER, subj_n - 1)),
            dma((chips - 1,)),
            dma((chips - 1,)),
            dma((chips - 1,)),
            dma((chips - 1,)),
        ],
        compiler_params=pltpu.CompilerParams(
            collective_id=0, has_side_effects=True, vmem_limit_bytes=32 * 1024 * 1024
        ),
        cost_estimate=pl.CostEstimate(
            flops=flops, bytes_accessed=data.size * 2, transcendentals=0
        ),
    )(data, shared_start)


def solution(mesh):
    placed = (P("subj", None, "vox"), P())
    body = functools.partial(local, mesh.shape["subj"], mesh.shape["vox"])
    return jax.shard_map(
        body, mesh=mesh, in_specs=placed, out_specs=(P("subj", None, None), P()), check_vma=False
    )
```

time: 157 us -> 43.3 us (0.28)
  blocking collectives: 78.7 us -> 0 us
  waiting for transfers between devices: 47.9 us -> 0 us
  Pallas kernels: 0 us -> 37.8 us
  matrix products: 14.6 us -> 0 us
  between operations: 14.2 us -> 0.65 us
  local copies, waits for them, and re-layouts: 1.45 us -> 4.61 us
    psum x2 -> x0, blocking collectives: 54.3 us -> none  [from_frames(): total = lax.psum(jnp.sum(share, axis=0), 'subj') / jnp.float32(subjects)]
    psum x1 -> x0, waiting for transfers between devices: 47.9 us -> none  [local(): lax.psum(jnp.einsum('stv,suv->stu', data, data, preferred_element_type=jn...]
    pallas_call x0 -> x1, Pallas kernels: none -> 37.8 us  [local(): pl.pallas_call(functools.partial(kernel, cores, subj_n, vox_n, chunk, own...]
    all_gather x3 -> x0, blocking collectives: 24.4 us -> none  [the longest x2 16.1 us: from_frames(): lax.all_gather(total, 'vox', axis=1, tiled=True)]
    dot_general x25 -> x0, matrix products: 14.6 us -> none  [the longest x1 5.31 us: local(): jnp.einsum('stv,suv->stu', data, data, preferred_element_type=jnp.float32)]
    unnamed x6 -> x3, local copies, waits for them, and re-layouts: 1.38 us -> 3.04 us
    pallas_call x0 -> x2, local copies, waits for them, and re-layouts: none -> 1.57 us  [local(): pl.pallas_call(functools.partial(kernel, cores, subj_n, vox_n, chunk, own...]
  transfers between devices with their start and end apart: 1 -> 0, of which waited for: 1 -> 0; matrix products, arithmetic and copies ran while one was open for 0% -> 0% of each run, Pallas kernels for 0% -> 0%
where the time goes in v1:
time: 43.3 us; the launch traced here: 43.1 us
  Pallas kernels  37.8 us (87%)
  local copies, waits for them, and re-layouts  4.61 us (11%)
  between operations  0.65 us (2%)
    pallas_call x1, Pallas kernels, local(): pl.pallas_call(functools.partial(kernel, cores, subj_n, vox_n, chunk, own...  37.8 us
    unnamed x3, local copies, waits for them, and re-layouts  3.04 us
    pallas_call x2, local copies, waits for them, and re-layouts, local(): pl.pallas_call(functools.partial(kernel, cores, subj_n, vox_n, chunk, own...  1.57 us

profile of v1, /device:TPU:0, one launch (start us, length us, event | category | flops | bytes accessed | tf_op | source)
XLA Modules:
  0.0 43.1 jit_solution(18131030674417656582)
XLA Ops:
  0.6 0.9 %copy.4.shared_ref = bf16[128,240]{1,0:T(8,128)(2,1)S(1)} copy(bf16[128,240]{0,1:T(8,128)(2,1)} %param.3) | data formatting | bytes 122880 | tf_op args[1]
  1.6 0.0 copy-start
  1.6 2.1 %copy-done = bf16[2,240,4096]{2,1,0:T(8,128)(2,1)S(1)} copy-done((bf16[2,240,4096]{2,1,0:T(8,128)(2,1)S(1)}, bf16[2,240,4096]{2,1,0:T(8,128)(2,1)}, u32[]{:S(2)}) %copy-start) | copy-done | bytes 3932184
  3.7 37.8 %shard_map.41 = (f32[2,128,240]{2,1,0:T(8,128)S(1)}, f32[128,240]{1,0:T(8,128)S(1)}) custom-call(bf16[2,240,4096]{2,1,0:T(8,128)(2,1)S(1)} %copy-done, bf16[128,240]{1,0:T(8,128)(2,1)S(1)} %copy.4.shared_ref), custom_call_target="tpu_custom_call" | custom-call | flops 943718400 | bytes 3932160 | tf_op jit(solution)/shard_map/pallas_call | solution.py:327
  41.5 0.8 %copy.5 = f32[2,128,240]{1,2,0:T(8,128)} copy(f32[2,128,240]{2,1,0:T(8,128)S(1)} %get-tuple-element.2) | data formatting | bytes 491520 | tf_op jit(solution)/shard_map/pallas_call | solution.py:327
  42.3 0.7 %copy.6 = f32[128,240]{0,1:T(8,128)} copy(f32[128,240]{1,0:T(8,128)S(1)} %get-tuple-element.3) | data formatting | bytes 245760 | tf_op jit(solution)/shard_map/pallas_call | solution.py:327
Async XLA Ops:
  1.6 2.1 %copy-start = (bf16[2,240,4096]{2,1,0:T(8,128)(2,1)S(1)}, bf16[2,240,4096]{2,1,0:T(8,128)(2,1)}, u32[]{:S(2)}) copy-start(bf16[2,240,4096]{2,1,0:T(8,128)(2,1)} %data_ref.1) | copy-start | bytes 11796484

commit v2 on v1

--- a/solution.py
+++ b/solution.py
@@ -10,7 +10,7 @@
 OUTER = 2
 LANES = 128
 ROWS = 16
-PIECES = 4
+PIECES = 1
 MESH = pl.DeviceIdType.MESH
 
 
@@ -107,12 +107,12 @@
 def kernel(
     cores, subj_n, vox_n, chunk, subjects,
     data_ref, shared_ref, proj_ref, resp_ref,
-    held, acc, packed, parts, gathered, tiles, sums, shares, pieces, proj_buf,
-    load_sem, out_sem, rs_send, rs_recv, ag_send, ag_recv, sum_send, sum_recv, share_send, share_recv,
+    held, acc, packed, parts, gathered, tiles, sums, shares, pieces,
+    load_sem, rs_send, rs_recv, ag_send, ag_recv, sum_send, sum_recv, share_send, share_recv,
     piece_send, piece_recv,
 ):
     own, frames, voxels = data_ref.shape
-    features = shared_ref.shape[0]
+    features = shared_ref.shape[1]
     s = lax.axis_index("subj")
     v = lax.axis_index("vox")
     z = s // cores
@@ -123,15 +123,21 @@
     tile_n = (features // ROWS) * 2
     mine = chip
 
-    def subj_device(step):
-        return (lax.rem(s + step, subj_n), v)
-
-    def chip_device(step):
+    def remember(count, work):
+        known = [None] + [work(step) for step in range(1, count)] if count <= 17 else None
+        return lambda step: known[step] if known else work(step)
+
+    def chip_at(step):
         other = lax.rem(chip + step, chips)
         return (other // vox_n * cores + core, lax.rem(other, vox_n))
 
-    def vox_device(step):
-        return (s, lax.rem(v + step, vox_n))
+    subj_device = remember(subj_n, lambda step: (lax.rem(s + step, subj_n), v))
+    chip_device = remember(chips, chip_at)
+    vox_device = remember(vox_n, lambda step: (s, lax.rem(v + step, vox_n)))
+    tile_of = remember(
+        subj_n,
+        lambda step: jnp.minimum(lax.rem(s + step, subj_n) // cores * vox_n + v, tile_n - 1),
+    )
 
     width = voxels // PIECES
     loads = []
@@ -154,6 +160,10 @@
 
     each(1, subj_n, greet_subj)
     each(1, chips, greet_chip)
+
+    shared = shared_ref[...].astype(jnp.float32).T.astype(jnp.bfloat16)
+    pad = jnp.zeros((features, 2 * LANES - frames), jnp.bfloat16)
+    shared = jnp.concatenate([shared, pad], axis=1)
 
     def scatter(i, step):
         other = lax.rem(v + step, vox_n)
@@ -178,8 +188,7 @@
         )
 
     def sum_copy(o, step):
-        other = lax.rem(s + step, subj_n)
-        tile = jnp.minimum(other // cores * vox_n + v, tile_n - 1)
+        tile = tile_of(step)
         return pltpu.make_async_remote_copy(
             src_ref=tiles.at[o, tile],
             dst_ref=sums.at[o, s],
@@ -233,10 +242,6 @@
         each(1, vox_n, lambda step: gather(i, step).wait_recv())
         grams.append(halves(unpack(gathered[i], frames)))
 
-    shared = shared_ref[...]
-    pad = jnp.zeros((features, 2 * LANES - frames), jnp.bfloat16)
-    shared = jnp.concatenate([shared, pad], axis=1)
-
     for o in range(OUTER):
         projections = chain(shared, grams)
         total = projections[0]
@@ -257,9 +262,7 @@
         each(1, subj_n, send_sum)
         if o == OUTER - 1:
             for i in range(own):
-                proj_buf[i] = projections[i][:, :frames]
-            writing = pltpu.make_async_copy(proj_buf, proj_ref, out_sem)
-            writing.start()
+                proj_ref[i] = projections[i].T[:frames]
 
         def reduce():
             sums[o, s] = tiles[o, mine]
@@ -289,7 +292,7 @@
             ],
             axis=0,
         )
-    resp_ref[...] = shared[:, :frames]
+    resp_ref[...] = shared.T[:frames]
 
     for i in range(own):
         each(1, vox_n, lambda step: scatter(i, step).wait_send())
@@ -308,7 +311,6 @@
             mine < tile_n,
             lambda: each(1, chips, lambda step: share_copy(o, step).wait_send()),
         )
-    writing.wait()
 
 
 def local(subj_n, vox_n, data, shared_start):
@@ -324,14 +326,14 @@
     f32, bf16 = jnp.float32, jnp.bfloat16
     dma = pltpu.SemaphoreType.DMA
     flops = 2 * own * frames * frames * voxels
-    return pl.pallas_call(
+    projections, response = pl.pallas_call(
         functools.partial(kernel, cores, subj_n, vox_n, chunk, own * subj_n),
         out_shape=(
-            jax.ShapeDtypeStruct((own, features, frames), f32),
-            jax.ShapeDtypeStruct((features, frames), f32),
+            jax.ShapeDtypeStruct((own, frames, features), f32),
+            jax.ShapeDtypeStruct((frames, features), f32),
         ),
         in_specs=[hbm, vmem],
-        out_specs=(hbm, vmem),
+        out_specs=(vmem, vmem),
         scratch_shapes=[
             pltpu.VMEM((own, frames, voxels), bf16),
             pltpu.VMEM((frames, frames), f32),
@@ -342,9 +344,7 @@
             pltpu.VMEM((OUTER, subj_n, ROWS, LANES), f32),
             pltpu.VMEM((tile_n, ROWS, LANES), bf16),
             pltpu.VMEM((tile_n, ROWS, LANES), f32),
-            pltpu.VMEM((own, features, frames), f32),
             dma((own, PIECES)),
-            dma,
             dma((own, vox_n - 1)),
             dma((own, vox_n - 1)),
             dma((own, vox_n - 1)),
@@ -357,12 +357,13 @@
             dma((chips - 1,)),
         ],
         compiler_params=pltpu.CompilerParams(
-            collective_id=0, has_side_effects=True, vmem_limit_bytes=32 * 1024 * 1024
+            collective_id=0, has_side_effects=True, vmem_limit_bytes=52 * 2**20
         ),
         cost_estimate=pl.CostEstimate(
             flops=flops, bytes_accessed=data.size * 2, transcendentals=0
         ),
-    )(data, shared_start)
+    )(data, shared_start.T)
+    return projections.transpose(0, 2, 1), response.T
 
 
 def solution(mesh):

time: 43.3 us -> 40.2 us (0.928)
  local copies, waits for them, and re-layouts: 4.61 us -> 2.17 us
  Pallas kernels: 37.8 us -> 37.2 us
    pallas_call x2 -> x0, local copies, waits for them, and re-layouts: 1.57 us -> none  [local(): pl.pallas_call(functools.partial(kernel, cores, subj_n, vox_n, chunk, own...]
    unnamed x3 -> x4, local copies, waits for them, and re-layouts: 3.04 us -> 2.17 us
    pallas_call x1, Pallas kernels: 37.8 us -> 37.2 us  [local(): pl.pallas_call(functools.partial(kernel, cores, subj_n, vox_n, chunk, own...]
where the time goes in v2:
time: 40.2 us; the launch traced here: 40 us
  Pallas kernels  37.2 us (93%)
  local copies, waits for them, and re-layouts  2.17 us (5%)
  between operations  0.65 us (2%)
    pallas_call x1, Pallas kernels, local(): pl.pallas_call(functools.partial(kernel, cores, subj_n, vox_n, chunk, own...  37.2 us
    unnamed x4, local copies, waits for them, and re-layouts  2.17 us

profile of v2, /device:TPU:0, one launch (start us, length us, event | category | flops | bytes accessed | tf_op | source)
XLA Modules:
  0.0 40.0 jit_solution(13269281916694594186)
XLA Ops:
  0.6 0.0 copy-start
  0.6 0.8 %copy-done = bf16[128,240]{0,1:T(8,128)(2,1)S(1)} copy-done((bf16[128,240]{0,1:T(8,128)(2,1)S(1)}, bf16[128,240]{0,1:T(8,128)(2,1)}, u32[]{:S(2)}) %copy-start) | copy-done | bytes 61464
  1.5 37.2 %shard_map.41 = (f32[2,240,128]{2,1,0:T(8,128)S(1)}, f32[240,128]{1,0:T(8,128)S(1)}) custom-call(bf16[2,240,4096]{2,1,0:T(8,128)(2,1)} %data_ref.1, bf16[240,128]{1,0:T(8,128)(2,1)S(1)} %bitcast.5), custom_call_target="tpu_custom_call" | custom-call | flops 943718400 | bytes 3932160 | tf_op jit(solution)/shard_map/pallas_call | solution.py:329
  38.6 0.7 %copy.6 = f32[2,128,240]{1,2,0:T(8,128)} copy(f32[2,128,240]{1,2,0:T(8,128)S(1)} %bitcast.3) | data formatting | bytes 491520
  39.3 0.6 %copy.7 = f32[128,240]{0,1:T(8,128)} copy(f32[128,240]{0,1:T(8,128)S(1)} %bitcast.4) | data formatting | bytes 245760
Async XLA Ops:
  0.6 0.8 %copy-start = (bf16[128,240]{0,1:T(8,128)(2,1)S(1)}, bf16[128,240]{0,1:T(8,128)(2,1)}, u32[]{:S(2)}) copy-start(bf16[128,240]{0,1:T(8,128)(2,1)} %param.3) | copy-start | bytes 184324

commit v3 on v2

--- a/solution.py
+++ b/solution.py
@@ -107,8 +107,8 @@
 def kernel(
     cores, subj_n, vox_n, chunk, subjects,
     data_ref, shared_ref, proj_ref, resp_ref,
-    held, acc, packed, parts, gathered, tiles, sums, shares, pieces,
-    load_sem, rs_send, rs_recv, ag_send, ag_recv, sum_send, sum_recv, share_send, share_recv,
+    held, acc, packed, parts, gathered, tiles, pair, sums, shares, pieces,
+    load_sem, rs_send, rs_recv, ag_send, ag_recv, pair_send, pair_recv, sum_send, sum_recv, share_send, share_recv,
     piece_send, piece_recv,
 ):
     own, frames, voxels = data_ref.shape
@@ -118,26 +118,28 @@
     z = s // cores
     core = s % cores
     planes = subj_n // cores
-    chips = planes * vox_n
-    chip = z * vox_n + v
     tile_n = (features // ROWS) * 2
-    mine = chip
+    block_n = tiles.shape[1]
+    joined = tile_n // block_n
+    plane_n = vox_n * cores
+    place = v * cores + core
+    mine = jnp.minimum(place, block_n - 1)
+    theirs = jnp.minimum(v * cores + 1 - core, block_n - 1)
 
     def remember(count, work):
         known = [None] + [work(step) for step in range(1, count)] if count <= 17 else None
         return lambda step: known[step] if known else work(step)
 
-    def chip_at(step):
-        other = lax.rem(chip + step, chips)
-        return (other // vox_n * cores + core, lax.rem(other, vox_n))
-
-    subj_device = remember(subj_n, lambda step: (lax.rem(s + step, subj_n), v))
-    chip_device = remember(chips, chip_at)
+    def plane_at(step):
+        other = lax.rem(place + step, plane_n)
+        return (z * cores + lax.rem(other, cores), other // cores)
+
+    plane_device = remember(plane_n, plane_at)
+    depth_device = remember(
+        planes, lambda step: (lax.rem(z + step, planes) * cores + core, v)
+    )
     vox_device = remember(vox_n, lambda step: (s, lax.rem(v + step, vox_n)))
-    tile_of = remember(
-        subj_n,
-        lambda step: jnp.minimum(lax.rem(s + step, subj_n) // cores * vox_n + v, tile_n - 1),
-    )
+    pair_device = (z * cores + 1 - core, v)
 
     width = voxels // PIECES
     loads = []
@@ -152,14 +154,14 @@
 
     barrier = pltpu.get_barrier_semaphore()
 
-    def greet_subj(step):
-        pl.semaphore_signal(barrier, inc=1, device_id=subj_device(step), device_id_type=MESH)
-
-    def greet_chip(step):
-        pl.semaphore_signal(barrier, inc=1, device_id=chip_device(step), device_id_type=MESH)
-
-    each(1, subj_n, greet_subj)
-    each(1, chips, greet_chip)
+    def greet_plane(step):
+        pl.semaphore_signal(barrier, inc=1, device_id=plane_device(step), device_id_type=MESH)
+
+    def greet_depth(step):
+        pl.semaphore_signal(barrier, inc=1, device_id=depth_device(step), device_id_type=MESH)
+
+    each(1, plane_n, greet_plane)
+    each(1, planes, greet_depth)
 
     shared = shared_ref[...].astype(jnp.float32).T.astype(jnp.bfloat16)
     pad = jnp.zeros((features, 2 * LANES - frames), jnp.bfloat16)
@@ -187,31 +189,39 @@
             device_id_type=MESH,
         )
 
-    def sum_copy(o, step):
-        tile = tile_of(step)
-        return pltpu.make_async_remote_copy(
-            src_ref=tiles.at[o, tile],
-            dst_ref=sums.at[o, s],
+    def pair_copy(o):
+        return pltpu.make_async_remote_copy(
+            src_ref=tiles.at[o, theirs],
+            dst_ref=pair.at[o],
+            send_sem=pair_send.at[o],
+            recv_sem=pair_recv.at[o],
+            device_id=pair_device,
+            device_id_type=MESH,
+        )
+
+    def depth_copy(o, step):
+        return pltpu.make_async_remote_copy(
+            src_ref=sums.at[o, z],
+            dst_ref=sums.at[o, z],
             send_sem=sum_send.at[o, step - 1],
             recv_sem=sum_recv.at[o, step - 1],
-            device_id=subj_device(step),
+            device_id=depth_device(step),
             device_id_type=MESH,
         )
 
     def share_copy(o, step):
         ref = pieces if o else shares
-        tile = jnp.minimum(mine, tile_n - 1)
-        return pltpu.make_async_remote_copy(
-            src_ref=ref.at[tile],
-            dst_ref=ref.at[tile],
+        return pltpu.make_async_remote_copy(
+            src_ref=ref.at[mine],
+            dst_ref=ref.at[mine],
             send_sem=(piece_send if o else share_send).at[step - 1],
             recv_sem=(piece_recv if o else share_recv).at[step - 1],
-            device_id=chip_device(step),
+            device_id=plane_device(step),
             device_id_type=MESH,
         )
 
     def when(condition, body):
-        if chips <= tile_n:
+        if plane_n <= block_n:
             body()
         else:
             pl.when(condition)(body)
@@ -226,7 +236,7 @@
                 acc[...] += dot_t(piece, piece)
         packed[i] = pack(acc[...], frames, vox_n * chunk)
         if i == 0:
-            pl.semaphore_wait(barrier, subj_n - 1 + chips - 1)
+            pl.semaphore_wait(barrier, plane_n - 1 + planes - 1)
         each(1, vox_n, lambda step: scatter(i, step).start())
 
     for i in range(own):
@@ -242,52 +252,53 @@
         each(1, vox_n, lambda step: gather(i, step).wait_recv())
         grams.append(halves(unpack(gathered[i], frames)))
 
+    def piece_of(ref, j):
+        return ref[j // joined, j % joined * ROWS : (j % joined + 1) * ROWS]
+
     for o in range(OUTER):
         projections = chain(shared, grams)
         total = projections[0]
         for other in projections[1:]:
             total = total + other
         for j in range(tile_n):
-            tiles[o, j] = total[
+            tiles[o, j // joined, j % joined * ROWS : (j % joined + 1) * ROWS] = total[
                 j // 2 * ROWS : (j // 2 + 1) * ROWS, j % 2 * LANES : (j % 2 + 1) * LANES
             ]
 
-        def send_sum(step):
-            other = lax.rem(s + step, subj_n)
-            when(
-                other // cores * vox_n + v < tile_n,
-                lambda: sum_copy(o, step).start(),
-            )
-
-        each(1, subj_n, send_sum)
+        when(place < block_n, lambda: pair_copy(o).start())
+        def stack():
+            pair_copy(o).wait_recv()
+            sums[o, z] = tiles[o, mine] + pair[o]
+            each(1, planes, lambda step: depth_copy(o, step).start())
+
+        when(place < block_n, stack)
         if o == OUTER - 1:
             for i in range(own):
                 proj_ref[i] = projections[i].T[:frames]
 
         def reduce():
-            sums[o, s] = tiles[o, mine]
-            each(1, subj_n, lambda step: sum_copy(o, step).wait_recv())
+            each(1, planes, lambda step: depth_copy(o, step).wait_recv())
             summed = sums[o, 0]
-            for q in range(1, subj_n):
+            for q in range(1, planes):
                 summed = summed + sums[o, q]
             mean = summed / jnp.float32(subjects)
             if o == OUTER - 1:
                 pieces[mine] = mean
             else:
                 shares[mine] = mean.astype(jnp.bfloat16)
-            each(1, chips, lambda step: share_copy(o, step).start())
-
-        when(mine < tile_n, reduce)
+            each(1, plane_n, lambda step: share_copy(o, step).start())
+
+        when(place < block_n, reduce)
 
         def wait_share(step):
-            other = lax.rem(chip + chips - step, chips)
-            when(other < tile_n, lambda: share_copy(o, step).wait_recv())
-
-        each(1, chips, wait_share)
+            other = lax.rem(place + plane_n - step, plane_n)
+            when(other < block_n, lambda: share_copy(o, step).wait_recv())
+
+        each(1, plane_n, wait_share)
         ref = pieces if o == OUTER - 1 else shares
         shared = jnp.concatenate(
             [
-                jnp.concatenate([ref[2 * a], ref[2 * a + 1]], axis=1)
+                jnp.concatenate([piece_of(ref, 2 * a), piece_of(ref, 2 * a + 1)], axis=1)
                 for a in range(tile_n // 2)
             ],
             axis=0,
@@ -299,27 +310,24 @@
         each(1, vox_n, lambda step: gather(i, step).wait_send())
     for o in range(OUTER):
 
-        def sent_sum(step):
-            other = lax.rem(s + step, subj_n)
-            when(
-                other // cores * vox_n + v < tile_n,
-                lambda: sum_copy(o, step).wait_send(),
-            )
-
-        each(1, subj_n, sent_sum)
-        when(
-            mine < tile_n,
-            lambda: each(1, chips, lambda step: share_copy(o, step).wait_send()),
-        )
+        def sent():
+            pair_copy(o).wait_send()
+            each(1, planes, lambda step: depth_copy(o, step).wait_send())
+            each(1, plane_n, lambda step: share_copy(o, step).wait_send())
+
+        when(place < block_n, sent)
 
 
 def local(subj_n, vox_n, data, shared_start):
     own, frames, voxels = data.shape
     features = shared_start.shape[0]
     cores = 2
-    chips = subj_n // cores * vox_n
+    planes = subj_n // cores
+    plane_n = vox_n * cores
     tile_n = features // ROWS * 2
-    assert chips >= tile_n and tile_n % vox_n == 0
+    joined = max(1, tile_n // plane_n)
+    assert tile_n % joined == 0 and tile_n // joined <= plane_n
+    blocks = (tile_n // joined, joined * ROWS, LANES)
     chunk = -(-frames // (8 * vox_n)) * 8
     hbm = pl.BlockSpec(memory_space=pltpu.HBM)
     vmem = pl.BlockSpec(memory_space=pltpu.VMEM)
@@ -340,21 +348,24 @@
             pltpu.VMEM((own, vox_n * chunk, LANES), f32),
             pltpu.VMEM((own, vox_n - 1, chunk, LANES), f32),
             pltpu.VMEM((own, vox_n * chunk, LANES), f32),
-            pltpu.VMEM((OUTER, tile_n, ROWS, LANES), f32),
-            pltpu.VMEM((OUTER, subj_n, ROWS, LANES), f32),
-            pltpu.VMEM((tile_n, ROWS, LANES), bf16),
-            pltpu.VMEM((tile_n, ROWS, LANES), f32),
+            pltpu.VMEM((OUTER, *blocks), f32),
+            pltpu.VMEM((OUTER, *blocks[1:]), f32),
+            pltpu.VMEM((OUTER, planes, *blocks[1:]), f32),
+            pltpu.VMEM(blocks, bf16),
+            pltpu.VMEM(blocks, f32),
             dma((own, PIECES)),
             dma((own, vox_n - 1)),
             dma((own, vox_n - 1)),
             dma((own, vox_n - 1)),
             dma((own, vox_n - 1)),
-            dma((OUTER, subj_n - 1)),
-            dma((OUTER, subj_n - 1)),
-            dma((chips - 1,)),
-            dma((chips - 1,)),
-            dma((chips - 1,)),
-            dma((chips - 1,)),
+            dma((OUTER,)),
+            dma((OUTER,)),
+            dma((OUTER, planes - 1)),
+            dma((OUTER, planes - 1)),
+            dma((plane_n - 1,)),
+            dma((plane_n - 1,)),
+            dma((plane_n - 1,)),
+            dma((plane_n - 1,)),
         ],
         compiler_params=pltpu.CompilerParams(
             collective_id=0, has_side_effects=True, vmem_limit_bytes=52 * 2**20

time: 40.2 us -> 36.6 us (0.910)
  Pallas kernels: 37.2 us -> 33.6 us
    pallas_call x1, Pallas kernels: 37.2 us -> 33.6 us  [local(): pl.pallas_call(functools.partial(kernel, cores, subj_n, vox_n, chunk, own...]
where the time goes in v3:
time: 36.6 us; the launch traced here: 36.4 us
  Pallas kernels  33.6 us (92%)
  local copies, waits for them, and re-layouts  2.17 us (6%)
  between operations  0.65 us (2%)
    pallas_call x1, Pallas kernels, local(): pl.pallas_call(functools.partial(kernel, cores, subj_n, vox_n, chunk, own...  33.6 us
    unnamed x4, local copies, waits for them, and re-layouts  2.17 us

profile of v3, /device:TPU:0, one launch (start us, length us, event | category | flops | bytes accessed | tf_op | source)
XLA Modules:
  0.0 36.4 jit_solution(17499958741291340968)
XLA Ops:
  0.6 0.0 copy-start
  0.6 0.8 %copy-done = bf16[128,240]{0,1:T(8,128)(2,1)S(1)} copy-done((bf16[128,240]{0,1:T(8,128)(2,1)S(1)}, bf16[128,240]{0,1:T(8,128)(2,1)}, u32[]{:S(2)}) %copy-start) | copy-done | bytes 61464
  1.5 33.6 %shard_map.41 = (f32[2,240,128]{2,1,0:T(8,128)S(1)}, f32[240,128]{1,0:T(8,128)S(1)}) custom-call(bf16[2,240,4096]{2,1,0:T(8,128)(2,1)} %data_ref.1, bf16[240,128]{1,0:T(8,128)(2,1)S(1)} %bitcast.5), custom_call_target="tpu_custom_call" | custom-call | flops 943718400 | bytes 3932160 | tf_op jit(solution)/shard_map/pallas_call | solution.py:337
  35.1 0.7 %copy.6 = f32[2,128,240]{1,2,0:T(8,128)} copy(f32[2,128,240]{1,2,0:T(8,128)S(1)} %bitcast.3) | data formatting | bytes 491520
  35.8 0.6 %copy.7 = f32[128,240]{0,1:T(8,128)} copy(f32[128,240]{0,1:T(8,128)S(1)} %bitcast.4) | data formatting | bytes 245760
Async XLA Ops:
  0.6 0.8 %copy-start = (bf16[128,240]{0,1:T(8,128)(2,1)S(1)}, bf16[128,240]{0,1:T(8,128)(2,1)}, u32[]{:S(2)}) copy-start(bf16[128,240]{0,1:T(8,128)(2,1)} %param.3) | copy-start | bytes 184324

commit v4 on v3

--- a/solution.py
+++ b/solution.py
@@ -272,10 +272,6 @@
             each(1, planes, lambda step: depth_copy(o, step).start())
 
         when(place < block_n, stack)
-        if o == OUTER - 1:
-            for i in range(own):
-                proj_ref[i] = projections[i].T[:frames]
-
         def reduce():
             each(1, planes, lambda step: depth_copy(o, step).wait_recv())
             summed = sums[o, 0]
@@ -293,6 +289,10 @@
         def wait_share(step):
             other = lax.rem(place + plane_n - step, plane_n)
             when(other < block_n, lambda: share_copy(o, step).wait_recv())
+
+        if o == OUTER - 1:
+            for i in range(own):
+                proj_ref[i] = projections[i].T[:frames]
 
         each(1, plane_n, wait_share)
         ref = pieces if o == OUTER - 1 else shares

time: 36.6 us -> 36.6 us (level)
  no operation moved by 1% of the time
where the time goes in v4:
time: 36.6 us; the launch traced here: 36.5 us
  Pallas kernels  33.6 us (92%)
  local copies, waits for them, and re-layouts  2.17 us (6%)
  between operations  0.65 us (2%)
    pallas_call x1, Pallas kernels, local(): pl.pallas_call(functools.partial(kernel, cores, subj_n, vox_n, chunk, own...  33.6 us
    unnamed x4, local copies, waits for them, and re-layouts  2.17 us

profile of v4, /device:TPU:0, one launch (start us, length us, event | category | flops | bytes accessed | tf_op | source)
XLA Modules:
  0.0 36.5 jit_solution(10988524240566231798)
XLA Ops:
  0.6 0.0 copy-start
  0.6 0.8 %copy-done = bf16[128,240]{0,1:T(8,128)(2,1)S(1)} copy-done((bf16[128,240]{0,1:T(8,128)(2,1)S(1)}, bf16[128,240]{0,1:T(8,128)(2,1)}, u32[]{:S(2)}) %copy-start) | copy-done | bytes 61464
  1.5 33.6 %shard_map.41 = (f32[2,240,128]{2,1,0:T(8,128)S(1)}, f32[240,128]{1,0:T(8,128)S(1)}) custom-call(bf16[2,240,4096]{2,1,0:T(8,128)(2,1)} %data_ref.1, bf16[240,128]{1,0:T(8,128)(2,1)S(1)} %bitcast.5), custom_call_target="tpu_custom_call" | custom-call | flops 943718400 | bytes 3932160 | tf_op jit(solution)/shard_map/pallas_call | solution.py:337
  35.1 0.7 %copy.6 = f32[2,128,240]{1,2,0:T(8,128)} copy(f32[2,128,240]{1,2,0:T(8,128)S(1)} %bitcast.3) | data formatting | bytes 491520
  35.8 0.6 %copy.7 = f32[128,240]{0,1:T(8,128)} copy(f32[128,240]{0,1:T(8,128)S(1)} %bitcast.4) | data formatting | bytes 245760
Async XLA Ops:
  0.6 0.8 %copy-start = (bf16[128,240]{0,1:T(8,128)(2,1)S(1)}, bf16[128,240]{0,1:T(8,128)(2,1)}, u32[]{:S(2)}) copy-start(bf16[128,240]{0,1:T(8,128)(2,1)} %param.3) | copy-start | bytes 184324
